TPU v7x, 256 devices: a whole 4x4x8 slice. The times are simulated.
256 devices in a mesh: dp: 8 (over z), tensor: 32 (over y, x, core).
Axes of the slice: x: 4, y: 4, z: 8, core: 2. Of those that a mesh axis runs over, the one named last changes fastest.
Arguments:
- gradient: bfloat16 [8, 4096, 14336], P('dp', None, 'tensor'), may hold values from -12 to 12
- feedback: bfloat16 [8, 4096, 14336], P('dp', None, 'tensor'), may hold values from -6 to 6
- right_prior: float32 [14336, 8], P('tensor'), may hold values from -6 to 6
Outputs:
- update: bfloat16 [4096, 14336], P('dp', 'tensor')
- new_feedback: bfloat16 [8, 4096, 14336], P('dp', None, 'tensor')
- right_next: float32 [14336, 8], P('tensor')
All inputs are finite; a program needn't handle non-finite values.
Results may differ from a plain program's by a relative error of at most 0.0011.
Values sent between devices are 32-bit elements; how exact they have to be, the bound alone decides.
No kernel may reach another device: no remote copies, remote signals or barrier semaphores. Data moves between devices by JAX's collectives and lax.ppermute only.
A program may use at most 64 MiB of HBM per device.

v0:
```python
import jax
import jax.numpy as jnp
from jax import lax
from jax.sharding import PartitionSpec as P

RANK = 8


def orthonormal_rows(matrix):
    basis = []
    for index in range(RANK):
        vector = matrix[index, :]
        for earlier in basis:
            vector = vector - jnp.dot(earlier, vector, precision=lax.Precision.HIGHEST) * earlier
        vector = vector * lax.rsqrt(jnp.sum(vector * vector) + 1e-06)
        basis.append(vector)
    return jnp.stack(basis, axis=0)


def shards(gradient, feedback, right_prior):
    corrected = gradient[0].astype(jnp.float32) + feedback[0].astype(jnp.float32)
    partial_value = lax.dot_general(
        right_prior, corrected, (((0,), (1,)), ((), ())), precision=lax.Precision.HIGHEST
    )
    left_rows = lax.psum(partial_value, ("dp", "tensor"))
    basis_rows = orthonormal_rows(left_rows)
    right_part = jnp.dot(basis_rows, corrected, precision=lax.Precision.HIGHEST)
    replicas = lax.axis_size("dp")
    right_rows = lax.psum(right_part, "dp") / replicas
    rebuilt = lax.dot_general(
        basis_rows, right_rows, (((0,), (0,)), ((), ())), precision=lax.Precision.HIGHEST
    )
    new_feedback = (corrected - rebuilt).astype(jnp.bfloat16)[None]
    slab_rows = rebuilt.shape[0] // replicas
    slab_start = lax.axis_index("dp") * slab_rows
    update = lax.dynamic_slice_in_dim(rebuilt, slab_start, slab_rows, 0).astype(jnp.bfloat16)
    return (update, new_feedback, right_rows.T)


def solution(mesh):
    placed = (P("dp", None, "tensor"), P("dp", None, "tensor"), P("tensor", None))
    return jax.shard_map(
        shards,
        mesh=mesh,
        in_specs=placed,
        out_specs=(P("dp", "tensor"), P("dp", None, "tensor"), P("tensor", None)),
        check_vma=False,
    )
```

profile of v0, /device:TPU:1, one launch (start us, length us, event | category | flops | bytes accessed | tf_op | source)
XLA Modules:
  0.0 375.8 jit_solution(8430722998579383274)
XLA Ops:
  7.2 0.7 copy-done
  7.9 8.2 %fusion.5 = f32[8,4096]{1,0:T(8,128)} fusion(f32[448,8]{0,1:T(8,128)S(1)} %copy-done, bf16[1,4096,448]{1,2,0:T(8,128)(2,1)} %param.4, bf16[1,4096,448]{1,2,0:T(8,128)(2,1)} %param.3), kind=kOutput, calls=%fused_computation.7 | convolution fusion | flops 181665792 | bytes 7485440 | tf_op jit(solution)/shard_map/dot_general | solution.py:22
  16.1 244.8 %all-reduce.2.cloned.1.call-done = f32[8,4096]{1,0:T(8,128)} async-done(((f32[8,4096]{1,0:T(8,128)}), f32[8,4096]{1,0:T(8,128)}) %all-reduce.2.cloned.1.call-update) | async-done | bytes 131088 | tf_op jit(solution)/shard_map/psum | solution.py:25
  260.9 1.5 multiply_reduce_fusion.35
  263.1 1.6 fusion.13
  264.8 0.7 multiply_reduce_fusion.6
  265.4 0.6 broadcast_multiply_fusion.6
  266.1 0.7 multiply_reduce_fusion.34
  267.4 6.0 %slice_subtract_fusion.4 = (f32[1,4096]{1,0:T(1,128)S(1)}, f32[1,4096]{1,0:T(1,128)S(1)}, f32[1,4096]{1,0:T(1,128)S(1)}, f32[1,4096]{1,0:T(1,128)S(1)}, f32[1,40...) fusion(f32[8,4096]{1,0:T(8,128)} %all-reduce.2.cloned.1.call-do, ...), kind=kLoop, calls=%fused_computation.90 | loop fusion | flops 61440 | bytes 344096 | tf_op jit(solution)/shard_map/sub | solution.py:14
  273.5 0.7 multiply_reduce_fusion.5
  274.2 1.2 multiply_reduce_fusion.33
  276.0 3.9 %multiply_subtract_fusion.16 = (f32[1,4096]{1,0:T(1,128)S(1)}, f32[1,4096]{1,0:T(1,128)S(1)}, f32[1,4096]{1,0:T(1,128)S(1)}, f32[1,4096]{1,0:T(1,128)S(1)}, f32[1,4096]{1,0:T(1,128)S(1)}, /*index=5*/f32[1,4096]{1,0:T(1,128)S(1)}) fusion(f32[1,4096]{1,0:T(1,128)S(1)} %get-tuple-element.50, f32[1,4096]{1,0:T(1,128)S(1)} %get-tuple-element.58, ...), kind=kLoop, calls=%fused_computation.62 | loop fusion | flops 53248 | bytes 213020 | tf_op jit(solution)/shard_map/sub | solution.py:14
  279.9 0.7 multiply_reduce_fusion.4
  280.6 1.9 multiply_reduce_fusion.32
  283.2 3.1 multiply_subtract_fusion.12
  286.2 0.7 multiply_reduce_fusion.3
  286.9 2.5 multiply_reduce_fusion.31
  290.2 2.5 multiply_subtract_fusion.7
  292.7 0.7 multiply_reduce_fusion.2
  293.4 5.1 %multiply_reduce_fusion.30 = f32[]{:T(128)} fusion(f32[4096]{0:T(1024)S(1)} %bitcast.70, f32[4096]{0:T(1024)S(1)} %bitcast.86, f32[4096]{0:T(1024)S(1)} %get-tuple-element.31, f32[4096]{0:T(1024)S(1)} %get-tuple-element.33, f32[4096]{0:T(1024)S(1)} %bitcast.65, f32[4096]{0:T(1024)S(1)} %bitcast.74, f32[4096]{0:T(1024)S(1)} %get-tuple-element.47, ...), kind=kLoop, calls=%fused_computation.52 | loop fusion | flops 90111 | bytes 114736 | tf_op jit(solution)/shard_map/reduce_sum | solution.py:15
  299.2 2.0 multiply_subtract_fusion.1
  301.1 0.7 multiply_reduce_fusion.1
  301.8 8.2 %multiply_reduce_fusion.29 = f32[]{:T(128)} fusion(f32[4096]{0:T(1024)S(1)} %bitcast.78, f32[4096]{0:T(1024)S(1)} %bitcast.91, f32[4096]{0:T(1024)S(1)} %bitcast.71, f32[4096]{0:T(1024)S(1)} %bitcast.87, f32[4096]{0:T(1024)S(1)} %get-tuple-element.31, f32[4096]{0:T(1024)S(1)} %get-tuple-element.33, f32[4096]{0:T(1024)S(1)} %bitcast.66, ...), kind=kLoop, calls=%fused_computation.45 | loop fusion | flops 139263 | bytes 147528 | tf_op jit(solution)/shard_map/reduce_sum | solution.py:15
  310.6 1.3 multiply_subtract_fusion
  311.9 0.6 multiply_reduce_fusion
  312.5 11.9 %multiply_reduce_fusion.28 = f32[]{:T(128)} fusion(f32[4096]{0:T(1024)S(1)} %bitcast.90, f32[4096]{0:T(1024)S(1)} %bitcast.120, f32[4096]{0:T(1024)S(1)} %bitcast.79, f32[4096]{0:T(1024)S(1)} %bitcast.92, f32[4096]{0:T(1024)S(1)} %bitcast.72, f32[4096]{0:T(1024)S(1)} %bitcast.88, f32[4096]{0:T(1024)S(1)} %get-tuple-element.31, ...), kind=kLoop, calls=%fused_computation.38 | loop fusion | flops 196607 | bytes 180324 | tf_op jit(solution)/shard_map/reduce_sum | solution.py:15
  325.9 8.3 %fusion = f32[8,448]{1,0:T(8,128)S(1)} fusion(f32[8,4096]{1,0:T(8,128)S(1)} %stack.2, bf16[1,4096,448]{1,2,0:T(8,128)(2,1)} %param.4, bf16[1,4096,448]{1,2,0:T(8,128)(2,1)} %param.3), kind=kOutput, calls=%fused_computation.1 | convolution fusion | flops 181665792 | bytes 7485440 | tf_op jit(solution)/shard_map/dot_general | solution.py:27
  334.2 21.7 %psum.15 = f32[8,448]{1,0:T(8,128)S(1)} all-reduce(f32[8,448]{1,0:T(8,128)S(1)} %fusion), channel_id=1, replica_groups=mesh['dp'=8,'tensor'=32] {'dp'}, use_global_device_ids=true, to_apply=%region_9.0 | all-reduce | flops 3584 | bytes 28672 | tf_op jit(solution)/shard_map/psum | solution.py:29
  355.8 0.6 multiply_bitcast_fusion
  356.4 5.9 %fusion.9 = f32[4096,448]{0,1:T(8,128)S(1)} fusion(f32[8,4096]{1,0:T(8,128)S(1)} %stack.2, f32[8,448]{1,0:T(8,128)S(1)} %psum.15), kind=kOutput, calls=%fused_computation.74 | convolution fusion | flops 176164352 | bytes 7485440 | tf_op jit(solution)/shard_map/dot_general | solution.py:30
  362.4 5.8 %fusion.8 = bf16[1,4096,448]{1,2,0:T(8,128)(2,1)} fusion(f32[4096,448]{0,1:T(8,128)S(1)} %fusion.9, bf16[1,4096,448]{1,2,0:T(8,128)(2,1)S(1)} %copy-done.1, bf16[1,4096,448]{1,2,0:T(8,128)(2,1)} %param.3), kind=kLoop, calls=%fused_computation.8 | loop fusion | flops 9175040 | bytes 18350080 | tf_op jit(solution)/shard_map/broadcast_in_dim | solution.py:33
  368.1 0.8 dynamic-slice_convert_fusion
  (7 shorter events, 0.8 us)
Async XLA Ops:
  7.2 0.7 copy-start
  7.2 253.7 %all-reduce.2.cloned.1.call-start = ((), (), s32[]{:S(2)}) async-start(), calls=%async_computation | async-start | bytes 262144 | tf_op jit(solution)/shard_map/psum | solution.py:25
  355.8 6.5 %copy-start.1 = (bf16[1,4096,448]{1,2,0:T(8,128)(2,1)S(1)}, bf16[1,4096,448]{1,2,0:T(8,128)(2,1)}, u32[]{:S(2)}) copy-start(bf16[1,4096,448]{1,2,0:T(8,128)(2,1)} %param.4) | copy-start | bytes 11010052
Sparse Core Ops, SparseCore 0:
  16.2 244.6 all-reduce.1
where the time goes:
time: 383 us; the launch traced here: 376 us
  waiting for transfers between devices  245 us (64%)
  other arithmetic  65.6 us (17%)
  matrix products  22.4 us (6%)
  blocking collectives  21.7 us (6%)
  between operations  19.6 us (5%)
    psum x1, waiting for transfers between devices, shards(): left_rows = lax.psum(partial_value, ('dp', 'tensor'))  245 us
    reduce_sum x8, other arithmetic, orthonormal_rows(): vector = vector * lax.rsqrt(jnp.sum(vector * vector) + 1e-06)  33 us
    psum x1, blocking collectives, shards(): right_rows = lax.psum(right_part, 'dp') / replicas  21.7 us
    sub x6, other arithmetic, orthonormal_rows(): vector - jnp.dot(earlier, vector, precision=lax.Precision.HIGHEST) * earlier  18.7 us
    dot_general x1, matrix products, shards(): right_part = jnp.dot(basis_rows, corrected, precision=lax.Precision.HIGHEST)  8.32 us
    dot_general x1, matrix products, shards(): lax.dot_general(right_prior, corrected, (((0,), (1,)), ((), ())), precisi...  8.19 us
  transfers between devices with their start and end apart: 1, of which 1 were waited for; matrix products, arithmetic and copies ran while one was open for 0% of the time, Pallas kernels for 0%

commit v1 on v0

v1 whole, which is shorter than its diff:
```python
import functools

import jax
import jax.numpy as jnp
from jax import lax
from jax.experimental import pallas as pl
from jax.experimental.pallas import tpu as pltpu
from jax.sharding import PartitionSpec as P

RANK = 8
LANES = 128
CHUNK = 512
F32 = jnp.float32
BF16 = jnp.bfloat16
LAST_BOTH = (((1,), (1,)), ((), ()))


def thirds(x):
    high = x.astype(BF16).astype(F32)
    rest = x - high
    middle = rest.astype(BF16).astype(F32)
    low = (rest - middle).astype(BF16).astype(F32)
    return high, middle, low


def fetches(sources, targets, sems):
    chunks = []
    for step in range(sources[0].shape[1] // CHUNK):
        columns = pl.ds(step * CHUNK, CHUNK)
        chunk = []
        for which, (source, target) in enumerate(zip(sources, targets)):
            copy = pltpu.make_async_copy(source.at[:, columns], target.at[:, columns], sems.at[which, step])
            copy.start()
            chunk.append(copy)
        chunks.append(chunk)
    return chunks


def left_kernel(prior, gradient_far, feedback_far, left, gradient, feedback, sems):
    chunks = fetches((gradient_far, feedback_far), (gradient, feedback), sems)
    terms = jnp.concatenate(thirds(prior[...]), axis=0).astype(BF16)
    for step, chunk in enumerate(chunks):
        columns = pl.ds(step * CHUNK, CHUNK)
        for copy in chunk:
            copy.wait()
        total = jnp.dot(terms, gradient[:, columns], preferred_element_type=F32)
        total += jnp.dot(terms, feedback[:, columns], preferred_element_type=F32)
        total = total[:RANK] + total[RANK : 2 * RANK] + total[2 * RANK :]
        for tile in range(CHUNK // LANES):
            left[step * (CHUNK // LANES) + tile] = total[:, tile * LANES : (tile + 1) * LANES]


def right_kernel(left, gradient_far, feedback_far, basis, right, gradient, feedback, sems):
    chunks = fetches((gradient_far, feedback_far), (gradient, feedback), sems)
    value = left[...]
    rank_row = lax.broadcasted_iota(jnp.int32, (RANK, 1), 0)
    scale = jnp.zeros((RANK, 1), F32)
    for column in range(RANK):
        row = value[:, column : column + 1, :]
        inner = jnp.sum(jnp.sum(value * row, axis=0), axis=1, keepdims=True)
        inverse = lax.rsqrt(inner[column : column + 1] + 1e-06)
        scale = jnp.where(rank_row == column, inverse, scale)
        if column < RANK - 1:
            factor = jnp.where(rank_row > column, inner * inverse * inverse, 0.0)
            value = value - factor[None] * row
    value = value * scale[None]
    for tile in range(value.shape[0]):
        lanes = pl.ds(tile * LANES, LANES)
        high, middle, low = thirds(value[tile])
        basis[0:RANK, lanes] = high
        basis[RANK : 2 * RANK, lanes] = middle
        basis[2 * RANK : 3 * RANK, lanes] = low
    total = jnp.zeros((3 * RANK, gradient.shape[0]), F32)
    for step, chunk in enumerate(chunks):
        columns = pl.ds(step * CHUNK, CHUNK)
        for copy in chunk:
            copy.wait()
        terms = basis[:, columns].astype(BF16)
        total += lax.dot_general(terms, gradient[:, columns], LAST_BOTH, preferred_element_type=F32)
        total += lax.dot_general(terms, feedback[:, columns], LAST_BOTH, preferred_element_type=F32)
    right[...] = total[:RANK] + total[RANK : 2 * RANK] + total[2 * RANK :]


def rebuild_kernel(
    replicas, rights, basis, gradient_far, feedback_far, update, residue, right_next, gradient, feedback, staged, slab, in_sems, sems
):
    chunks = fetches((gradient_far, feedback_far), (gradient, feedback), in_sems)
    mine = lax.axis_index("dp")
    wide = gradient.shape[1]
    total = rights[0]
    for replica in range(1, replicas):
        total = total + rights[replica]
    right = total * (1.0 / replicas)
    right_next[...] = right
    first, second, third = thirds(right)
    lhs = jnp.concatenate((first, first, first, second, second, third), axis=0).astype(BF16)
    copies = []
    for step, chunk in enumerate(chunks):
        columns = pl.ds(step * CHUNK, CHUNK)
        one, two, three = (basis[RANK * k : RANK * (k + 1), columns] for k in range(3))
        rhs = jnp.concatenate((one, two, three, one, two, one), axis=0).astype(BF16)
        rebuilt = lax.dot_general(lhs, rhs, (((0,), (0,)), ((), ())), preferred_element_type=F32)
        for copy in chunk:
            copy.wait()
        corrected = gradient[:, columns].astype(F32) + feedback[:, columns].astype(F32)
        staged[:, columns] = (corrected - rebuilt).astype(BF16)
        copy = pltpu.make_async_copy(staged.at[:, columns], residue.at[:, columns], sems.at[step])
        copy.start()
        copies.append(copy)

        @pl.when(mine == step)
        def _():
            slab[...] = rebuilt.astype(BF16)

    copy = pltpu.make_async_copy(slab, update, sems.at[wide // CHUNK])
    copy.start()
    copies.append(copy)
    for copy in copies:
        copy.wait()


def shards(gradient, feedback, right_prior):
    gradient, feedback = gradient[0].T, feedback[0].T
    units, wide = gradient.shape
    replicas, parts = lax.axis_size("dp"), lax.axis_size("tensor")
    steps = wide // CHUNK
    vmem = pl.BlockSpec(memory_space=pltpu.VMEM)
    hbm = pl.BlockSpec(memory_space=pltpu.HBM)
    held = [pltpu.VMEM((units, wide), BF16)] * 2
    arrived = pltpu.SemaphoreType.DMA((2, steps))
    params = pltpu.CompilerParams(vmem_limit_bytes=24 * 2**20)
    with jax.named_scope("left"):
        left = pl.pallas_call(
            left_kernel,
            out_shape=jax.ShapeDtypeStruct((wide // LANES, RANK, LANES), F32),
            in_specs=[vmem, hbm, hbm],
            out_specs=vmem,
            scratch_shapes=[*held, arrived],
            compiler_params=params,
        )(right_prior.T, gradient, feedback)
    with jax.named_scope("left_sum"):
        piece = jnp.sum(lax.all_to_all(left, "tensor", 0, 0), axis=0)
        pieces = jnp.broadcast_to(piece[None], (replicas,) + piece.shape)
        piece = jnp.sum(lax.all_to_all(pieces, "dp", 0, 0), axis=0)
        pieces = jnp.broadcast_to(piece[None], (parts,) + piece.shape)
        left = lax.all_to_all(pieces, "tensor", 0, 0)
    with jax.named_scope("right"):
        basis, right = pl.pallas_call(
            right_kernel,
            out_shape=(jax.ShapeDtypeStruct((3 * RANK, wide), F32), jax.ShapeDtypeStruct((RANK, units), F32)),
            in_specs=[vmem, hbm, hbm],
            out_specs=[vmem, vmem],
            scratch_shapes=[*held, arrived],
            compiler_params=params,
        )(left, gradient, feedback)
    with jax.named_scope("right_sum"):
        rights = lax.all_to_all(jnp.broadcast_to(right[None], (replicas,) + right.shape), "dp", 0, 0)
    with jax.named_scope("rebuild"):
        update, residue, right_next = pl.pallas_call(
            functools.partial(rebuild_kernel, replicas),
            out_shape=(
                jax.ShapeDtypeStruct((units, CHUNK), BF16),
                jax.ShapeDtypeStruct((units, wide), BF16),
                jax.ShapeDtypeStruct((RANK, units), F32),
            ),
            in_specs=[vmem, vmem, hbm, hbm],
            out_specs=[hbm, hbm, vmem],
            scratch_shapes=[
                *held,
                pltpu.VMEM((units, wide), BF16),
                pltpu.VMEM((units, CHUNK), BF16),
                arrived,
                pltpu.SemaphoreType.DMA((steps + 1,)),
            ],
            compiler_params=params,
        )(rights, basis, gradient, feedback)
    return update.T, residue.T[None], right_next.T


def solution(mesh):
    placed = (P("dp", None, "tensor"), P("dp", None, "tensor"), P("tensor", None))
    return jax.shard_map(
        shards,
        mesh=mesh,
        in_specs=placed,
        out_specs=(P("dp", "tensor"), P("dp", None, "tensor"), P("tensor", None)),
        check_vma=False,
    )
```

time: 383 us -> 78.6 us (0.21); the launches traced: 376 us -> 78.2 us
  waiting for transfers between devices: 245 us -> 0 us
  other arithmetic: 65.6 us -> 0.05 us
  blocking collectives: 21.7 us -> 54.3 us
  matrix products: 22.4 us -> 0 us
  between operations: 19.6 us -> 0.67 us
  Pallas kernels: 0 us -> 14.2 us
  local copies, waits for them, and re-layouts: 1.7 us -> 8.9 us
    psum x1 -> x0, waiting for transfers between devices: 245 us -> none  [shards(): left_rows = lax.psum(partial_value, ('dp', 'tensor'))]
    all_to_all x0 -> x4, blocking collectives: none -> 54.3 us  [the longest x1 16 us: shards(): piece = jnp.sum(lax.all_to_all(left, 'tensor', 0, 0), axis=0)]
    reduce_sum x8 -> x2, other arithmetic: 33 us -> 0.05 us  [the longest x1 0.04 us: shards(): piece = jnp.sum(lax.all_to_all(left, 'tensor', 0, 0), axis=0)]
    dot_general x3 -> x0, matrix products: 22.4 us -> none  [the longest x1 8.32 us: shards(): right_part = jnp.dot(basis_rows, corrected, precision=lax.Precision.HIGHEST)]
    psum x1 -> x0, blocking collectives: 21.7 us -> none  [shards(): right_rows = lax.psum(right_part, 'dp') / replicas]
    sub x6 -> x0, other arithmetic: 18.7 us -> none  [orthonormal_rows(): vector - jnp.dot(earlier, vector, precision=lax.Precision.HIGHEST) * earlier]
    pallas_call x0 -> x3, Pallas kernels: none -> 14.2 us  [the longest x1 5.89 us: shards(): pl.pallas_call(functools.partial(rebuild_kernel, replicas), out_shape=(ja...]
    unnamed x4 -> x10, local copies, waits for them, and re-layouts: 0.67 us -> 8.86 us
  transfers between devices with their start and end apart: 1 -> 0, of which waited for: 1 -> 0; matrix products, arithmetic and copies ran while one was open for 0% -> 0% of each run, Pallas kernels for 0% -> 0%
where the time goes in v1:
time: 78.6 us; the launch traced here: 78.2 us
  blocking collectives  54.3 us (69%)
  Pallas kernels  14.2 us (18%)
  local copies, waits for them, and re-layouts  8.9 us (11%)
    all_to_all x1, blocking collectives, shards(): piece = jnp.sum(lax.all_to_all(left, 'tensor', 0, 0), axis=0)  16 us
    all_to_all x1, blocking collectives, shards(): piece = jnp.sum(lax.all_to_all(pieces, 'dp', 0, 0), axis=0)  15 us
    all_to_all x1, blocking collectives, shards(): left = lax.all_to_all(pieces, 'tensor', 0, 0)  12.6 us
    all_to_all x1, blocking collectives, shards(): lax.all_to_all(jnp.broadcast_to(right[None], (replicas,) + right.shape),...  10.8 us
    unnamed x10, local copies, waits for them, and re-layouts  8.86 us
    pallas_call x1, Pallas kernels, shards(): pl.pallas_call(functools.partial(rebuild_kernel, replicas), out_shape=(ja...  5.89 us
    pallas_call x1, Pallas kernels, shards(): pl.pallas_call(right_kernel, out_shape=(jax.ShapeDtypeStruct((3 * RANK, w...  5.49 us
    pallas_call x1, Pallas kernels, shards(): pl.pallas_call(left_kernel, out_shape=jax.ShapeDtypeStruct((wide // LANES...  2.85 us

profile of v1, /device:TPU:1, one launch (start us, length us, event | category | flops | bytes accessed | tf_op | source)
XLA Modules:
  0.0 78.2 jit_solution(1768643747685978045)
XLA Ops:
  0.6 0.0 copy-start
  0.6 2.0 %copy-done = bf16[1,4096,448]{1,2,0:T(8,128)(2,1)S(1)} copy-done((bf16[1,4096,448]{1,2,0:T(8,128)(2,1)S(1)}, bf16[1,4096,448]{1,2,0:T(8,128)(2,1)}, u32[]{:S(2)}) %copy-start) | copy-done | bytes 3670040
  2.7 0.0 copy-start.2
  2.7 2.0 %copy-done.2 = bf16[1,4096,448]{1,2,0:T(8,128)(2,1)S(1)} copy-done((bf16[1,4096,448]{1,2,0:T(8,128)(2,1)S(1)}, bf16[1,4096,448]{1,2,0:T(8,128)(2,1)}, u32[]{:S(2)}) %copy-start.2) | copy-done | bytes 3670040
  4.7 0.0 copy-start.4
  4.7 0.7 copy-done.4
  5.4 2.8 %left.1 = f32[32,8,128]{2,1,0:T(8,128)S(1)} custom-call(f32[8,448]{1,0:T(8,128)S(1)} %bitcast.18, bf16[448,4096]{1,0:T(8,128)(2,1)S(1)} %bitcast.12, bf16[448,4096]{1,0:T(8,128)(2,1)S(1)} %bitcast.15), custom_call_target="tpu_custom_call" | custom-call | tf_op jit(solution)/shard_map/left/pallas_call | solution.py:133
  8.3 16.0 %all_to_all.20 = f32[32,8,128]{2,1,0:T(8,128)S(1)} all-to-all(f32[32,8,128]{2,1,0:T(8,128)S(1)} %left.1), channel_id=1, replica_groups=mesh['dp'=8,'tensor'=32] {'tensor'}, dimensions={0} | all-to-all | bytes 262144 | tf_op jit(solution)/shard_map/left_sum/all_to_all | solution.py:142
  24.3 15.0 %all_to_all.21 = f32[8,8,128]{2,1,0:T(8,128)S(1)} all-to-all(f32[8,8,128]{2,1,0:T(8,128)S(1)} %broadcast_in_dim.8), channel_id=1, replica_groups=mesh['dp'=8,'tensor'=32] {'dp'}, dimensions={0} | all-to-all | bytes 65536 | tf_op jit(solution)/shard_map/left_sum/all_to_all | solution.py:144
  39.3 12.6 %all_to_all.22.left = f32[32,8,128]{2,1,0:T(8,128)S(1)} all-to-all(f32[32,8,128]{2,1,0:T(8,128)S(1)} %broadcast_in_dim.9), channel_id=1, replica_groups=mesh['dp'=8,'tensor'=32] {'tensor'}, dimensions={0} | all-to-all | bytes 262144 | tf_op jit(solution)/shard_map/left_sum/all_to_all | solution.py:146
  51.9 0.0 copy-start.1
  51.9 2.0 %copy-done.1 = bf16[1,4096,448]{1,2,0:T(8,128)(2,1)S(1)} copy-done((bf16[1,4096,448]{1,2,0:T(8,128)(2,1)S(1)}, bf16[1,4096,448]{1,2,0:T(8,128)(2,1)}, u32[]{:S(2)}) %copy-start.1) | copy-done | bytes 3670040
  54.0 0.0 copy-start.3
  54.0 2.0 %copy-done.3 = bf16[1,4096,448]{1,2,0:T(8,128)(2,1)S(1)} copy-done((bf16[1,4096,448]{1,2,0:T(8,128)(2,1)S(1)}, bf16[1,4096,448]{1,2,0:T(8,128)(2,1)}, u32[]{:S(2)}) %copy-start.3) | copy-done | bytes 3670040
  56.0 5.5 %right.1 = (f32[24,4096]{1,0:T(8,128)S(1)}, f32[8,448]{1,0:T(8,128)S(1)}) custom-call(f32[32,8,128]{2,1,0:T(8,128)S(1)} %all_to_all.22.left, bf16[448,4096]{1,0:T(8,128)(2,1)S(1)} %bitcast.13, bf16[448,4096]{1,0:T(8,128)(2,1)S(1)} %bitcast.16), custom_call_target="tpu_custom_call" | custom-call | tf_op jit(solution)/shard_map/right/pallas_call | solution.py:148
  61.5 10.8 %all_to_all.23.rights = f32[8,8,448]{2,1,0:T(8,128)S(1)} all-to-all(f32[8,8,448]{2,1,0:T(8,128)S(1)} %broadcast_in_dim.10), channel_id=1, replica_groups=mesh['dp'=8,'tensor'=32] {'dp'}, dimensions={0} | all-to-all | bytes 229376 | tf_op jit(solution)/shard_map/right_sum/all_to_all | solution.py:157
  72.3 5.9 %rebuild.1 = (bf16[448,512]{1,0:T(8,128)(2,1)}, bf16[448,4096]{1,0:T(8,128)(2,1)}, f32[8,448]{1,0:T(8,128)}) custom-call(f32[8,8,448]{2,1,0:T(8,128)S(1)} %all_to_all.23.rights, f32[24,4096]{1,0:T(8,128)S(1)} %get-tuple-element.9.basis, bf16[448,4096]{1,0:T(8,128)(2,1)S(1)} %bitcast.14, bf16[448,4096]{1,0:T(8,128)(2,1)S(1)} %bitcast.17), custom_call_target="tpu_custom_call" | custom-call | tf_op jit(solution)/shard_map/rebuild/pallas_call | solution.py:159
  (5 shorter events, 0.1 us)
Async XLA Ops:
  0.6 2.0 %copy-start = (bf16[1,4096,448]{1,2,0:T(8,128)(2,1)S(1)}, bf16[1,4096,448]{1,2,0:T(8,128)(2,1)}, u32[]{:S(2)}) copy-start(bf16[1,4096,448]{1,2,0:T(8,128)(2,1)} %param.3) | copy-start | bytes 11010052
  2.7 2.0 %copy-start.2 = (bf16[1,4096,448]{1,2,0:T(8,128)(2,1)S(1)}, bf16[1,4096,448]{1,2,0:T(8,128)(2,1)}, u32[]{:S(2)}) copy-start(bf16[1,4096,448]{1,2,0:T(8,128)(2,1)} %param.4) | copy-start | bytes 11010052
  4.7 0.7 copy-start.4
  51.9 2.0 %copy-start.1 = (bf16[1,4096,448]{1,2,0:T(8,128)(2,1)S(1)}, bf16[1,4096,448]{1,2,0:T(8,128)(2,1)}, u32[]{:S(2)}) copy-start(bf16[1,4096,448]{1,2,0:T(8,128)(2,1)} %param.3) | copy-start | bytes 11010052
  54.0 2.0 %copy-start.3 = (bf16[1,4096,448]{1,2,0:T(8,128)(2,1)S(1)}, bf16[1,4096,448]{1,2,0:T(8,128)(2,1)}, u32[]{:S(2)}) copy-start(bf16[1,4096,448]{1,2,0:T(8,128)(2,1)} %param.4) | copy-start | bytes 11010052

commit v2 on v1

v2 whole, which is shorter than its diff:
```python
import functools

import jax
import jax.numpy as jnp
from jax import lax
from jax.experimental import pallas as pl
from jax.experimental.pallas import tpu as pltpu
from jax.sharding import PartitionSpec as P

RANK = 8
LANES = 128
CHUNK = 512
F32 = jnp.float32
BF16 = jnp.bfloat16
LAST_BOTH = (((1,), (1,)), ((), ()))


def thirds(x):
    high = x.astype(BF16).astype(F32)
    rest = x - high
    middle = rest.astype(BF16).astype(F32)
    low = (rest - middle).astype(BF16).astype(F32)
    return high, middle, low


def left_kernel(prior_far, gradient_far, feedback_far, left, gradient, feedback, prior, sems):
    steps = gradient.shape[1] // CHUNK
    prior_copy = pltpu.make_async_copy(prior_far, prior, sems.at[2, 0])
    prior_copy.start()
    chunks = []
    for step in range(steps):
        columns = pl.ds(step * CHUNK, CHUNK)
        chunk = []
        for which, (source, target) in enumerate(((gradient_far, gradient), (feedback_far, feedback))):
            copy = pltpu.make_async_copy(source.at[:, columns], target.at[:, columns], sems.at[which, step])
            copy.start()
            chunk.append(copy)
        chunks.append(chunk)
    prior_copy.wait()
    terms = jnp.concatenate(thirds(prior[...]), axis=0).astype(BF16)
    for step, chunk in enumerate(chunks):
        columns = pl.ds(step * CHUNK, CHUNK)
        for copy in chunk:
            copy.wait()
        total = jnp.dot(terms, gradient[:, columns], preferred_element_type=F32)
        total += jnp.dot(terms, feedback[:, columns], preferred_element_type=F32)
        total = total[:RANK] + total[RANK : 2 * RANK] + total[2 * RANK :]
        for tile in range(CHUNK // LANES):
            left[step * (CHUNK // LANES) + tile] = total[:, tile * LANES : (tile + 1) * LANES]


def spread_kernel(pieces, copies):
    total = pieces[0]
    for piece in range(1, pieces.shape[0]):
        total = total + pieces[piece]
    for copy in range(copies.shape[0]):
        copies[copy] = total


def right_kernel(left, gradient, feedback, basis, right):
    value = left[...]
    rank_row = lax.broadcasted_iota(jnp.int32, (RANK, 1), 0)
    scale = jnp.zeros((RANK, 1), F32)
    for column in range(RANK):
        row = value[:, column : column + 1, :]
        inner = jnp.sum(jnp.sum(value * row, axis=0), axis=1, keepdims=True)
        inverse = lax.rsqrt(inner[column : column + 1] + 1e-06)
        scale = jnp.where(rank_row == column, inverse, scale)
        if column < RANK - 1:
            factor = jnp.where(rank_row > column, inner * inverse * inverse, 0.0)
            value = value - factor[None] * row
    value = value * scale[None]
    for tile in range(value.shape[0]):
        lanes = pl.ds(tile * LANES, LANES)
        high, middle, low = thirds(value[tile])
        basis[0:RANK, lanes] = high
        basis[RANK : 2 * RANK, lanes] = middle
        basis[2 * RANK : 3 * RANK, lanes] = low
    terms = basis[...].astype(BF16)
    total = lax.dot_general(terms, gradient[...], LAST_BOTH, preferred_element_type=F32)
    total += lax.dot_general(terms, feedback[...], LAST_BOTH, preferred_element_type=F32)
    total = total[:RANK] + total[RANK : 2 * RANK] + total[2 * RANK :]
    for copy in range(right.shape[0]):
        right[copy] = total


def rebuild_kernel(
    replicas, rights, basis, gradient, feedback, update, residue, right_next, staged, slab, sems
):
    mine = lax.axis_index("dp")
    wide = gradient.shape[1]
    total = rights[0]
    for replica in range(1, replicas):
        total = total + rights[replica]
    right = total * (1.0 / replicas)
    right_next[...] = right
    first, second, third = thirds(right)
    lhs = jnp.concatenate((first, first, first, second, second, third), axis=0).astype(BF16)
    copies = []
    for step in range(wide // CHUNK):
        columns = pl.ds(step * CHUNK, CHUNK)
        one, two, three = (basis[RANK * k : RANK * (k + 1), columns] for k in range(3))
        rhs = jnp.concatenate((one, two, three, one, two, one), axis=0).astype(BF16)
        rebuilt = lax.dot_general(lhs, rhs, (((0,), (0,)), ((), ())), preferred_element_type=F32)
        corrected = gradient[:, columns].astype(F32) + feedback[:, columns].astype(F32)
        staged[:, columns] = (corrected - rebuilt).astype(BF16)
        copy = pltpu.make_async_copy(staged.at[:, columns], residue.at[:, columns], sems.at[step])
        copy.start()
        copies.append(copy)

        @pl.when(mine == step)
        def _():
            slab[...] = rebuilt.astype(BF16)

    copy = pltpu.make_async_copy(slab, update, sems.at[wide // CHUNK])
    copy.start()
    copies.append(copy)
    for copy in copies:
        copy.wait()


def shards(gradient, feedback, right_prior):
    gradient, feedback = gradient[0].T, feedback[0].T
    units, wide = gradient.shape
    replicas, parts = lax.axis_size("dp"), lax.axis_size("tensor")
    steps = wide // CHUNK
    vmem = pl.BlockSpec(memory_space=pltpu.VMEM)
    hbm = pl.BlockSpec(memory_space=pltpu.HBM)
    held = pltpu.VMEM((units, wide), BF16)
    params = pltpu.CompilerParams(vmem_limit_bytes=16 * 2**20)
    tile = (RANK, LANES)

    def spread(pieces, count):
        return pl.pallas_call(
            spread_kernel,
            out_shape=jax.ShapeDtypeStruct((count,) + tile, F32),
            in_specs=[vmem],
            out_specs=vmem,
            compiler_params=pltpu.CompilerParams(vmem_limit_bytes=2**20),
        )(pieces)

    with jax.named_scope("left"):
        left, gradient, feedback = pl.pallas_call(
            left_kernel,
            out_shape=(jax.ShapeDtypeStruct((wide // LANES,) + tile, F32), held, held),
            in_specs=[hbm, hbm, hbm],
            out_specs=[vmem, vmem, vmem],
            scratch_shapes=[pltpu.VMEM((RANK, units), F32), pltpu.SemaphoreType.DMA((3, steps))],
            compiler_params=params,
        )(*(pltpu.with_memory_space_constraint(x, pltpu.HBM) for x in (right_prior.T, gradient, feedback)))
    with jax.named_scope("left_sum"):
        pieces = spread(lax.all_to_all(left, "tensor", 0, 0), replicas)
        pieces = spread(lax.all_to_all(pieces, "dp", 0, 0), parts)
        left = lax.all_to_all(pieces, "tensor", 0, 0)
    with jax.named_scope("right"):
        basis, right = pl.pallas_call(
            right_kernel,
            out_shape=(jax.ShapeDtypeStruct((3 * RANK, wide), F32), jax.ShapeDtypeStruct((replicas, RANK, units), F32)),
            in_specs=[vmem, vmem, vmem],
            out_specs=[vmem, vmem],
            compiler_params=params,
        )(left, gradient, feedback)
    with jax.named_scope("right_sum"):
        rights = lax.all_to_all(right, "dp", 0, 0)
    with jax.named_scope("rebuild"):
        update, residue, right_next = pl.pallas_call(
            functools.partial(rebuild_kernel, replicas),
            out_shape=(
                jax.ShapeDtypeStruct((units, CHUNK), BF16),
                jax.ShapeDtypeStruct((units, wide), BF16),
                jax.ShapeDtypeStruct((RANK, units), F32),
            ),
            in_specs=[vmem, vmem, vmem, vmem],
            out_specs=[hbm, hbm, vmem],
            scratch_shapes=[
                pltpu.VMEM((units, wide), BF16),
                pltpu.VMEM((units, CHUNK), BF16),
                pltpu.SemaphoreType.DMA((steps + 1,)),
            ],
            compiler_params=params,
        )(rights, basis, gradient, feedback)
    return update.T, residue.T[None], right_next.T


def solution(mesh):
    placed = (P("dp", None, "tensor"), P("dp", None, "tensor"), P("tensor", None))
    return jax.shard_map(
        shards,
        mesh=mesh,
        in_specs=placed,
        out_specs=(P("dp", "tensor"), P("dp", None, "tensor"), P("tensor", None)),
        check_vma=False,
    )
```

time: 78.6 us -> 65.8 us (0.84)
  local copies, waits for them, and re-layouts: 8.9 us -> 0 us
  Pallas kernels: 14.2 us -> 10.5 us
    unnamed x10 -> x0, local copies, waits for them, and re-layouts: 8.86 us -> none
    pallas_call x1, Pallas kernels: 5.49 us -> 3.07 us  [shards(): pl.pallas_call(right_kernel, out_shape=(jax.ShapeDtypeStruct((3 * RANK, w...]
    pallas_call x1, Pallas kernels: 5.89 us -> 3.72 us  [shards(): pl.pallas_call(functools.partial(rebuild_kernel, replicas), out_shape=(ja...]
    pallas_call x1 -> x3, Pallas kernels: 2.85 us -> 3.68 us  [the longest x1 3.63 us: shards(): pl.pallas_call(left_kernel, out_shape=(jax.ShapeDtypeStruct((wide // LANE...]
where the time goes in v2:
time: 65.8 us; the launch traced here: 65.5 us
  blocking collectives  54.3 us (83%)
  Pallas kernels  10.5 us (16%)
    all_to_all x1, blocking collectives, shards(): pieces = spread(lax.all_to_all(left, 'tensor', 0, 0), replicas)  16 us
    all_to_all x1, blocking collectives, shards(): pieces = spread(lax.all_to_all(pieces, 'dp', 0, 0), parts)  15 us
    all_to_all x1, blocking collectives, shards(): left = lax.all_to_all(pieces, 'tensor', 0, 0)  12.6 us
    all_to_all x1, blocking collectives, shards(): rights = lax.all_to_all(right, 'dp', 0, 0)  10.8 us
    pallas_call x1, Pallas kernels, shards(): pl.pallas_call(functools.partial(rebuild_kernel, replicas), out_shape=(ja...  3.72 us
    pallas_call x1, Pallas kernels, shards(): pl.pallas_call(left_kernel, out_shape=(jax.ShapeDtypeStruct((wide // LANE...  3.63 us
    pallas_call x1, Pallas kernels, shards(): pl.pallas_call(right_kernel, out_shape=(jax.ShapeDtypeStruct((3 * RANK, w...  3.07 us

profile of v2, /device:TPU:1, one launch (start us, length us, event | category | flops | bytes accessed | tf_op | source)
XLA Modules:
  0.0 65.5 jit_solution(2043836572556104654)
XLA Ops:
  0.6 3.6 %left.1 = (f32[32,8,128]{2,1,0:T(8,128)S(1)}, bf16[448,4096]{1,0:T(8,128)(2,1)S(1)}, bf16[448,4096]{1,0:T(8,128)(2,1)S(1)}) custom-call(f32[8,448]{1,0:T(8,128)} %bitcast.14, bf16[448,4096]{1,0:T(8,128)(2,1)} %bitcast.12, bf16[448,4096]{1,0:T(8,128)(2,1)} %bitcast.13), custom_call_target="tpu_custom_call" | custom-call | tf_op jit(solution)/shard_map/left/pallas_call | solution.py:143
  4.3 16.0 %all_to_all.20.pieces = f32[32,8,128]{2,1,0:T(8,128)S(1)} all-to-all(f32[32,8,128]{2,1,0:T(8,128)S(1)} %get-tuple-element.11), channel_id=1, replica_groups=mesh['dp'=8,'tensor'=32] {'tensor'}, dimensions={0} | all-to-all | bytes 262144 | tf_op jit(solution)/shard_map/left_sum/all_to_all | solution.py:152
  20.3 15.0 %all_to_all.21.pieces = f32[8,8,128]{2,1,0:T(8,128)S(1)} all-to-all(f32[8,8,128]{2,1,0:T(8,128)S(1)} %left_sum.2), channel_id=1, replica_groups=mesh['dp'=8,'tensor'=32] {'dp'}, dimensions={0} | all-to-all | bytes 65536 | tf_op jit(solution)/shard_map/left_sum/all_to_all | solution.py:153
  35.3 12.6 %all_to_all.22.left = f32[32,8,128]{2,1,0:T(8,128)S(1)} all-to-all(f32[32,8,128]{2,1,0:T(8,128)S(1)} %left_sum.3), channel_id=1, replica_groups=mesh['dp'=8,'tensor'=32] {'tensor'}, dimensions={0} | all-to-all | bytes 262144 | tf_op jit(solution)/shard_map/left_sum/all_to_all | solution.py:154
  47.9 3.1 %right.1 = (f32[24,4096]{1,0:T(8,128)S(1)}, f32[8,8,448]{2,1,0:T(8,128)S(1)}) custom-call(f32[32,8,128]{2,1,0:T(8,128)S(1)} %all_to_all.22.left, bf16[448,4096]{1,0:T(8,128)(2,1)S(1)} %get-tuple-element.12.gradient, bf16[448,4096]{1,0:T(8,128)(2,1)S(1)} %get-tuple-element.13.feedback), custom_call_target="tpu_custom_call" | custom-call | tf_op jit(solution)/shard_map/right/pallas_call | solution.py:156
  51.0 10.8 %all_to_all.23.rights = f32[8,8,448]{2,1,0:T(8,128)S(1)} all-to-all(f32[8,8,448]{2,1,0:T(8,128)S(1)} %get-tuple-element.14), channel_id=1, replica_groups=mesh['dp'=8,'tensor'=32] {'dp'}, dimensions={0} | all-to-all | bytes 229376 | tf_op jit(solution)/shard_map/right_sum/all_to_all | solution.py:164
  61.7 3.7 %rebuild.1 = (bf16[448,512]{1,0:T(8,128)(2,1)}, bf16[448,4096]{1,0:T(8,128)(2,1)}, f32[8,448]{1,0:T(8,128)}) custom-call(f32[8,8,448]{2,1,0:T(8,128)S(1)} %all_to_all.23.rights, f32[24,4096]{1,0:T(8,128)S(1)} %get-tuple-element.15.basis, bf16[448,4096]{1,0:T(8,128)(2,1)S(1)} %get-tuple-element.12.gradient, bf16[448,4096]{1,0:T(8,128)(2,1)S(1)} %get-tuple-element.13.feedback), custom_call_target="tpu_custom_call" | custom-call | tf_op jit(solution)/shard_map/rebuild/pallas_call | solution.py:166
  (2 shorter events, 0.1 us)

commit v3 on v2

--- a/solution.py
+++ b/solution.py
@@ -13,6 +13,7 @@
 F32 = jnp.float32
 BF16 = jnp.bfloat16
 LAST_BOTH = (((1,), (1,)), ((), ()))
+FIRST_BOTH = (((0,), (0,)), ((), ()))
 
 
 def thirds(x):
@@ -23,28 +24,30 @@
     return high, middle, low
 
 
+def folded(total):
+    return total[:RANK] + total[RANK : 2 * RANK] + total[2 * RANK :]
+
+
 def left_kernel(prior_far, gradient_far, feedback_far, left, gradient, feedback, prior, sems):
     steps = gradient.shape[1] // CHUNK
     prior_copy = pltpu.make_async_copy(prior_far, prior, sems.at[2, 0])
     prior_copy.start()
-    chunks = []
     for step in range(steps):
         columns = pl.ds(step * CHUNK, CHUNK)
-        chunk = []
         for which, (source, target) in enumerate(((gradient_far, gradient), (feedback_far, feedback))):
             copy = pltpu.make_async_copy(source.at[:, columns], target.at[:, columns], sems.at[which, step])
             copy.start()
-            chunk.append(copy)
-        chunks.append(chunk)
     prior_copy.wait()
     terms = jnp.concatenate(thirds(prior[...]), axis=0).astype(BF16)
-    for step, chunk in enumerate(chunks):
-        columns = pl.ds(step * CHUNK, CHUNK)
-        for copy in chunk:
-            copy.wait()
+
+    @pl.loop(0, steps)
+    def _(step):
+        columns = pl.ds(pl.multiple_of(step * CHUNK, CHUNK), CHUNK)
+        for which, (source, target) in enumerate(((gradient_far, gradient), (feedback_far, feedback))):
+            pltpu.make_async_copy(source.at[:, columns], target.at[:, columns], sems.at[which, step]).wait()
         total = jnp.dot(terms, gradient[:, columns], preferred_element_type=F32)
         total += jnp.dot(terms, feedback[:, columns], preferred_element_type=F32)
-        total = total[:RANK] + total[RANK : 2 * RANK] + total[2 * RANK :]
+        total = folded(total)
         for tile in range(CHUNK // LANES):
             left[step * (CHUNK // LANES) + tile] = total[:, tile * LANES : (tile + 1) * LANES]
 
@@ -57,64 +60,79 @@
         copies[copy] = total
 
 
-def right_kernel(left, gradient, feedback, basis, right):
+def put_thirds(tiles, where):
+    for tile in range(tiles.shape[0]):
+        for third, part in enumerate(thirds(tiles[tile])):
+            where[third * RANK : (third + 1) * RANK, tile * LANES : (tile + 1) * LANES] = part
+
+
+def right_kernel(left, gradient, feedback, basis, right, left_terms):
+    put_thirds(left[...], left_terms)
+    terms = left_terms[...].astype(BF16)
+    product = lax.dot_general(terms, gradient[...], LAST_BOTH, preferred_element_type=F32)
+    product += lax.dot_general(terms, feedback[...], LAST_BOTH, preferred_element_type=F32)
+    product = folded(product)
     value = left[...]
     rank_row = lax.broadcasted_iota(jnp.int32, (RANK, 1), 0)
     scale = jnp.zeros((RANK, 1), F32)
+    tile = (RANK, LANES)
+    change = (lax.broadcasted_iota(jnp.int32, tile, 0) == lax.broadcasted_iota(jnp.int32, tile, 1)).astype(F32)
     for column in range(RANK):
         row = value[:, column : column + 1, :]
-        inner = jnp.sum(jnp.sum(value * row, axis=0), axis=1, keepdims=True)
+        products = value * row
+        count = products.shape[0]
+        while count > 1:
+            count //= 2
+            products = products[:count] + products[count : 2 * count]
+        inner = jnp.sum(products[0], axis=1, keepdims=True)
         inverse = lax.rsqrt(inner[column : column + 1] + 1e-06)
         scale = jnp.where(rank_row == column, inverse, scale)
         if column < RANK - 1:
             factor = jnp.where(rank_row > column, inner * inverse * inverse, 0.0)
             value = value - factor[None] * row
-    value = value * scale[None]
-    for tile in range(value.shape[0]):
-        lanes = pl.ds(tile * LANES, LANES)
-        high, middle, low = thirds(value[tile])
-        basis[0:RANK, lanes] = high
-        basis[RANK : 2 * RANK, lanes] = middle
-        basis[2 * RANK : 3 * RANK, lanes] = low
-    terms = basis[...].astype(BF16)
-    total = lax.dot_general(terms, gradient[...], LAST_BOTH, preferred_element_type=F32)
-    total += lax.dot_general(terms, feedback[...], LAST_BOTH, preferred_element_type=F32)
-    total = total[:RANK] + total[RANK : 2 * RANK] + total[2 * RANK :]
+            change = change - factor * change[column : column + 1]
+    put_thirds(value * scale[None], basis)
+    change = change * scale
+    total = change[:, 0:1] * product[0:1]
+    for column in range(1, RANK):
+        total = total + change[:, column : column + 1] * product[column : column + 1]
     for copy in range(right.shape[0]):
         right[copy] = total
 
 
 def rebuild_kernel(
-    replicas, rights, basis, gradient, feedback, update, residue, right_next, staged, slab, sems
+    replicas, rights, basis, gradient, feedback, update, residue, right_next, staged, slab, right, sems
 ):
     mine = lax.axis_index("dp")
     wide = gradient.shape[1]
+    steps = wide // CHUNK
     total = rights[0]
     for replica in range(1, replicas):
         total = total + rights[replica]
-    right = total * (1.0 / replicas)
-    right_next[...] = right
-    first, second, third = thirds(right)
+    total = total * (1.0 / replicas)
+    right[...] = total
+    copies = [pltpu.make_async_copy(right, right_next, sems.at[steps + 1])]
+    copies[0].start()
+    first, second, third = thirds(total)
     lhs = jnp.concatenate((first, first, first, second, second, third), axis=0).astype(BF16)
-    copies = []
-    for step in range(wide // CHUNK):
-        columns = pl.ds(step * CHUNK, CHUNK)
+
+    def rebuilt(columns):
         one, two, three = (basis[RANK * k : RANK * (k + 1), columns] for k in range(3))
         rhs = jnp.concatenate((one, two, three, one, two, one), axis=0).astype(BF16)
-        rebuilt = lax.dot_general(lhs, rhs, (((0,), (0,)), ((), ())), preferred_element_type=F32)
+        return lax.dot_general(lhs, rhs, FIRST_BOTH, preferred_element_type=F32)
+
+    for step in range(steps):
+        columns = pl.ds(step * CHUNK, CHUNK)
         corrected = gradient[:, columns].astype(F32) + feedback[:, columns].astype(F32)
-        staged[:, columns] = (corrected - rebuilt).astype(BF16)
+        staged[:, columns] = (corrected - rebuilt(columns)).astype(BF16)
         copy = pltpu.make_async_copy(staged.at[:, columns], residue.at[:, columns], sems.at[step])
         copy.start()
         copies.append(copy)
-
-        @pl.when(mine == step)
-        def _():
-            slab[...] = rebuilt.astype(BF16)
-
-    copy = pltpu.make_async_copy(slab, update, sems.at[wide // CHUNK])
-    copy.start()
-    copies.append(copy)
+        if step == 0:
+            slab[...] = rebuilt(pl.ds(pl.multiple_of(mine * CHUNK, CHUNK), CHUNK)).astype(BF16)
+            copy = pltpu.make_async_copy(slab, update, sems.at[steps])
+            copy.start()
+            copies.append(copy)
     for copy in copies:
         copy.wait()
 
@@ -144,7 +162,7 @@
             left_kernel,
             out_shape=(jax.ShapeDtypeStruct((wide // LANES,) + tile, F32), held, held),
             in_specs=[hbm, hbm, hbm],
-            out_specs=[vmem, vmem, vmem],
+            out_specs=[vmem] * 3,
             scratch_shapes=[pltpu.VMEM((RANK, units), F32), pltpu.SemaphoreType.DMA((3, steps))],
             compiler_params=params,
         )(*(pltpu.with_memory_space_constraint(x, pltpu.HBM) for x in (right_prior.T, gradient, feedback)))
@@ -158,6 +176,7 @@
             out_shape=(jax.ShapeDtypeStruct((3 * RANK, wide), F32), jax.ShapeDtypeStruct((replicas, RANK, units), F32)),
             in_specs=[vmem, vmem, vmem],
             out_specs=[vmem, vmem],
+            scratch_shapes=[pltpu.VMEM((3 * RANK, wide), F32)],
             compiler_params=params,
         )(left, gradient, feedback)
     with jax.named_scope("right_sum"):
@@ -170,12 +189,13 @@
                 jax.ShapeDtypeStruct((units, wide), BF16),
                 jax.ShapeDtypeStruct((RANK, units), F32),
             ),
-            in_specs=[vmem, vmem, vmem, vmem],
-            out_specs=[hbm, hbm, vmem],
+            in_specs=[vmem] * 4,
+            out_specs=[hbm] * 3,
             scratch_shapes=[
                 pltpu.VMEM((units, wide), BF16),
                 pltpu.VMEM((units, CHUNK), BF16),
-                pltpu.SemaphoreType.DMA((steps + 1,)),
+                pltpu.VMEM((RANK, units), F32),
+                pltpu.SemaphoreType.DMA((steps + 2,)),
             ],
             compiler_params=params,
         )(rights, basis, gradient, feedback)

time: 65.8 us -> 63.6 us (0.967)
  Pallas kernels: 10.5 us -> 8.31 us
    pallas_call x1, Pallas kernels: 3.72 us -> 2.42 us  [shards(): pl.pallas_call(functools.partial(rebuild_kernel, replicas), out_shape=(ja...]
    pallas_call x1, Pallas kernels: 3.07 us -> 2.2 us  [shards(): pl.pallas_call(right_kernel, out_shape=(jax.ShapeDtypeStruct((3 * RANK, w...]
where the time goes in v3:
time: 63.6 us; the launch traced here: 63.3 us
  blocking collectives  54.3 us (85%)
  Pallas kernels  8.31 us (13%)
  between operations  0.65 us (1%)
    all_to_all x1, blocking collectives, shards(): pieces = spread(lax.all_to_all(left, 'tensor', 0, 0), replicas)  16 us
    all_to_all x1, blocking collectives, shards(): pieces = spread(lax.all_to_all(pieces, 'dp', 0, 0), parts)  15 us
    all_to_all x1, blocking collectives, shards(): left = lax.all_to_all(pieces, 'tensor', 0, 0)  12.6 us
    all_to_all x1, blocking collectives, shards(): rights = lax.all_to_all(right, 'dp', 0, 0)  10.8 us
    pallas_call x1, Pallas kernels, shards(): pl.pallas_call(left_kernel, out_shape=(jax.ShapeDtypeStruct((wide // LANE...  3.63 us
    pallas_call x1, Pallas kernels, shards(): pl.pallas_call(functools.partial(rebuild_kernel, replicas), out_shape=(ja...  2.42 us
    pallas_call x1, Pallas kernels, shards(): pl.pallas_call(right_kernel, out_shape=(jax.ShapeDtypeStruct((3 * RANK, w...  2.2 us

profile of v3, /device:TPU:1, one launch (start us, length us, event | category | flops | bytes accessed | tf_op | source)
XLA Modules:
  0.0 63.3 jit_solution(17043944448136573259)
XLA Ops:
  0.6 3.6 %left.1 = (f32[32,8,128]{2,1,0:T(8,128)S(1)}, bf16[448,4096]{1,0:T(8,128)(2,1)S(1)}, bf16[448,4096]{1,0:T(8,128)(2,1)S(1)}) custom-call(f32[8,448]{1,0:T(8,128)} %bitcast.14, bf16[448,4096]{1,0:T(8,128)(2,1)} %bitcast.12, bf16[448,4096]{1,0:T(8,128)(2,1)} %bitcast.13), custom_call_target="tpu_custom_call" | custom-call | tf_op jit(solution)/shard_map/left/pallas_call | solution.py:161
  4.3 16.0 %all_to_all.20.pieces = f32[32,8,128]{2,1,0:T(8,128)S(1)} all-to-all(f32[32,8,128]{2,1,0:T(8,128)S(1)} %get-tuple-element.11), channel_id=1, replica_groups=mesh['dp'=8,'tensor'=32] {'tensor'}, dimensions={0} | all-to-all | bytes 262144 | tf_op jit(solution)/shard_map/left_sum/all_to_all | solution.py:170
  20.3 15.0 %all_to_all.21.pieces = f32[8,8,128]{2,1,0:T(8,128)S(1)} all-to-all(f32[8,8,128]{2,1,0:T(8,128)S(1)} %left_sum.2), channel_id=1, replica_groups=mesh['dp'=8,'tensor'=32] {'dp'}, dimensions={0} | all-to-all | bytes 65536 | tf_op jit(solution)/shard_map/left_sum/all_to_all | solution.py:171
  35.3 12.6 %all_to_all.22.left = f32[32,8,128]{2,1,0:T(8,128)S(1)} all-to-all(f32[32,8,128]{2,1,0:T(8,128)S(1)} %left_sum.3), channel_id=1, replica_groups=mesh['dp'=8,'tensor'=32] {'tensor'}, dimensions={0} | all-to-all | bytes 262144 | tf_op jit(solution)/shard_map/left_sum/all_to_all | solution.py:172
  47.9 2.2 %right.1 = (f32[24,4096]{1,0:T(8,128)S(1)}, f32[8,8,448]{2,1,0:T(8,128)S(1)}) custom-call(f32[32,8,128]{2,1,0:T(8,128)S(1)} %all_to_all.22.left, bf16[448,4096]{1,0:T(8,128)(2,1)S(1)} %get-tuple-element.12.gradient, bf16[448,4096]{1,0:T(8,128)(2,1)S(1)} %get-tuple-element.13.feedback), custom_call_target="tpu_custom_call" | custom-call | tf_op jit(solution)/shard_map/right/pallas_call | solution.py:174
  50.1 10.8 %all_to_all.23.rights = f32[8,8,448]{2,1,0:T(8,128)S(1)} all-to-all(f32[8,8,448]{2,1,0:T(8,128)S(1)} %get-tuple-element.14), channel_id=1, replica_groups=mesh['dp'=8,'tensor'=32] {'dp'}, dimensions={0} | all-to-all | bytes 229376 | tf_op jit(solution)/shard_map/right_sum/all_to_all | solution.py:183
  60.9 2.4 %rebuild.1 = (bf16[448,512]{1,0:T(8,128)(2,1)}, bf16[448,4096]{1,0:T(8,128)(2,1)}, f32[8,448]{1,0:T(8,128)}) custom-call(f32[8,8,448]{2,1,0:T(8,128)S(1)} %all_to_all.23.rights, f32[24,4096]{1,0:T(8,128)S(1)} %get-tuple-element.15.basis, bf16[448,4096]{1,0:T(8,128)(2,1)S(1)} %get-tuple-element.12.gradient, bf16[448,4096]{1,0:T(8,128)(2,1)S(1)} %get-tuple-element.13.feedback), custom_call_target="tpu_custom_call" | custom-call | tf_op jit(solution)/shard_map/rebuild/pallas_call | solution.py:185
  (2 shorter events, 0.1 us)

commit v4 on v3

--- a/solution.py
+++ b/solution.py
@@ -10,6 +10,8 @@
 RANK = 8
 LANES = 128
 CHUNK = 512
+SIDE = 4
+CORES = 2
 F32 = jnp.float32
 BF16 = jnp.bfloat16
 LAST_BOTH = (((1,), (1,)), ((), ()))
@@ -60,17 +62,15 @@
         copies[copy] = total
 
 
-def put_thirds(tiles, where):
-    for tile in range(tiles.shape[0]):
-        for third, part in enumerate(thirds(tiles[tile])):
-            where[third * RANK : (third + 1) * RANK, tile * LANES : (tile + 1) * LANES] = part
-
-
-def right_kernel(left, gradient, feedback, basis, right, left_terms):
-    put_thirds(left[...], left_terms)
-    terms = left_terms[...].astype(BF16)
-    product = lax.dot_general(terms, gradient[...], LAST_BOTH, preferred_element_type=F32)
-    product += lax.dot_general(terms, feedback[...], LAST_BOTH, preferred_element_type=F32)
+def right_kernel(left, gradient, feedback, basis, right):
+    block = CHUNK // LANES
+    product = jnp.zeros((3 * RANK, gradient.shape[0]), F32)
+    for step in range(gradient.shape[1] // CHUNK):
+        columns = pl.ds(step * CHUNK, CHUNK)
+        rows = jnp.concatenate([left[step * block + tile] for tile in range(block)], axis=1)
+        terms = jnp.concatenate(thirds(rows), axis=0).astype(BF16)
+        product += lax.dot_general(terms, gradient[:, columns], LAST_BOTH, preferred_element_type=F32)
+        product += lax.dot_general(terms, feedback[:, columns], LAST_BOTH, preferred_element_type=F32)
     product = folded(product)
     value = left[...]
     rank_row = lax.broadcasted_iota(jnp.int32, (RANK, 1), 0)
@@ -91,7 +91,11 @@
             factor = jnp.where(rank_row > column, inner * inverse * inverse, 0.0)
             value = value - factor[None] * row
             change = change - factor * change[column : column + 1]
-    put_thirds(value * scale[None], basis)
+    value = value * scale[None]
+    for tile in range(value.shape[0]):
+        one, two, three = thirds(value[tile])
+        rows = jnp.concatenate((one, two, three, one, two, one), axis=0)
+        basis[:, tile * LANES : (tile + 1) * LANES] = rows.astype(BF16)
     change = change * scale
     total = change[:, 0:1] * product[0:1]
     for column in range(1, RANK):
@@ -117,9 +121,7 @@
     lhs = jnp.concatenate((first, first, first, second, second, third), axis=0).astype(BF16)
 
     def rebuilt(columns):
-        one, two, three = (basis[RANK * k : RANK * (k + 1), columns] for k in range(3))
-        rhs = jnp.concatenate((one, two, three, one, two, one), axis=0).astype(BF16)
-        return lax.dot_general(lhs, rhs, FIRST_BOTH, preferred_element_type=F32)
+        return lax.dot_general(lhs, basis[:, columns], FIRST_BOTH, preferred_element_type=F32)
 
     for step in range(steps):
         columns = pl.ds(step * CHUNK, CHUNK)
@@ -137,6 +139,16 @@
         copy.wait()
 
 
+def plane_groups(replicas):
+    halves = [
+        [(y * SIDE + x) * CORES + core for x in pair for y in range(SIDE) for core in range(CORES)]
+        for pair in ((0, 1), (3, 2))
+    ]
+    parts = SIDE * SIDE * CORES
+    mixed = [[replica * parts + place for replica in range(replicas) for place in pair] for pair in zip(*halves)]
+    return halves, mixed
+
+
 def shards(gradient, feedback, right_prior):
     gradient, feedback = gradient[0].T, feedback[0].T
     units, wide = gradient.shape
@@ -151,7 +163,7 @@
     def spread(pieces, count):
         return pl.pallas_call(
             spread_kernel,
-            out_shape=jax.ShapeDtypeStruct((count,) + tile, F32),
+            out_shape=jax.ShapeDtypeStruct((count,) + pieces.shape[1:], F32),
             in_specs=[vmem],
             out_specs=vmem,
             compiler_params=pltpu.CompilerParams(vmem_limit_bytes=2**20),
@@ -166,17 +178,21 @@
             scratch_shapes=[pltpu.VMEM((RANK, units), F32), pltpu.SemaphoreType.DMA((3, steps))],
             compiler_params=params,
         )(*(pltpu.with_memory_space_constraint(x, pltpu.HBM) for x in (right_prior.T, gradient, feedback)))
+    halves, mixed = plane_groups(replicas)
+    members, reducers = len(halves[0]), len(mixed[0])
+    share = (wide // LANES // members,) + tile
     with jax.named_scope("left_sum"):
-        pieces = spread(lax.all_to_all(left, "tensor", 0, 0), replicas)
-        pieces = spread(lax.all_to_all(pieces, "dp", 0, 0), parts)
-        left = lax.all_to_all(pieces, "tensor", 0, 0)
+        pieces = left.reshape((members,) + share)
+        pieces = spread(lax.all_to_all(pieces, "tensor", 0, 0, axis_index_groups=halves), reducers)
+        pieces = spread(lax.all_to_all(pieces, ("dp", "tensor"), 0, 0, axis_index_groups=mixed), members)
+        left = lax.all_to_all(pieces, "tensor", 0, 0, axis_index_groups=halves)
+        left = left.reshape((wide // LANES,) + tile)
     with jax.named_scope("right"):
         basis, right = pl.pallas_call(
             right_kernel,
-            out_shape=(jax.ShapeDtypeStruct((3 * RANK, wide), F32), jax.ShapeDtypeStruct((replicas, RANK, units), F32)),
+            out_shape=(jax.ShapeDtypeStruct((6 * RANK, wide), BF16), jax.ShapeDtypeStruct((replicas, RANK, units), F32)),
             in_specs=[vmem, vmem, vmem],
             out_specs=[vmem, vmem],
-            scratch_shapes=[pltpu.VMEM((3 * RANK, wide), F32)],
             compiler_params=params,
         )(left, gradient, feedback)
     with jax.named_scope("right_sum"):

time: 63.6 us -> 62.4 us (0.981)
  blocking collectives: 54.3 us -> 53.1 us
    all_to_all x3, blocking collectives: 43.6 us -> 42.9 us  [the longest x1 19.3 us: shards(): lax.all_to_all(pieces, ('dp', 'tensor'), 0, 0, axis_index_groups=mixed)]
where the time goes in v4:
time: 62.4 us; the launch traced here: 62.1 us
  blocking collectives  53.1 us (85%)
  Pallas kernels  8.28 us (13%)
  between operations  0.66 us (1%)
    all_to_all x1, blocking collectives, shards(): lax.all_to_all(pieces, ('dp', 'tensor'), 0, 0, axis_index_groups=mixed)  19.3 us
    all_to_all x1, blocking collectives, shards(): lax.all_to_all(pieces, 'tensor', 0, 0, axis_index_groups=halves)  12.9 us
    all_to_all x1, blocking collectives, shards(): left = lax.all_to_all(pieces, 'tensor', 0, 0, axis_index_groups=halves)  10.7 us
    all_to_all x1, blocking collectives, shards(): rights = lax.all_to_all(right, 'dp', 0, 0)  10.2 us
    pallas_call x1, Pallas kernels, shards(): pl.pallas_call(left_kernel, out_shape=(jax.ShapeDtypeStruct((wide // LANE...  3.63 us
    pallas_call x1, Pallas kernels, shards(): pl.pallas_call(functools.partial(rebuild_kernel, replicas), out_shape=(ja...  2.42 us
    pallas_call x1, Pallas kernels, shards(): pl.pallas_call(right_kernel, out_shape=(jax.ShapeDtypeStruct((6 * RANK, w...  2.18 us

profile of v4, /device:TPU:1, one launch (start us, length us, event | category | flops | bytes accessed | tf_op | source)
XLA Modules:
  0.0 62.1 jit_solution(8172970725904273503)
XLA Ops:
  0.6 3.6 %left.1 = (f32[32,8,128]{2,1,0:T(8,128)S(1)}, bf16[448,4096]{1,0:T(8,128)(2,1)S(1)}, bf16[448,4096]{1,0:T(8,128)(2,1)S(1)}) custom-call(f32[8,448]{1,0:T(8,128)} %bitcast.18, bf16[448,4096]{1,0:T(8,128)(2,1)} %bitcast.16, bf16[448,4096]{1,0:T(8,128)(2,1)} %bitcast.17), custom_call_target="tpu_custom_call" | custom-call | tf_op jit(solution)/shard_map/left/pallas_call | solution.py:173
  4.3 12.9 %all_to_all.20.pieces = f32[16,2,8,128]{3,2,1,0:T(8,128)S(1)} all-to-all(f32[16,2,8,128]{3,2,1,0:T(8,128)S(1)} %bitcast.15), channel_id=1, replica_groups={{0,1,8,9,16,17,24,25,2,3,10,11,18,19,26,27},{6,7,14,15,22,23,30,31,4,5,..., dimensions={0} | all-to-all | bytes 262144 | tf_op jit(solution)/shard_map/left_sum/all_to_all | solution.py:186
  17.2 19.3 %all_to_all.21.pieces = f32[16,2,8,128]{3,2,1,0:T(8,128)S(1)} all-to-all(f32[16,2,8,128]{3,2,1,0:T(8,128)S(1)} %left_sum.2), channel_id=1, replica_groups={{0,6,32,38,64,70,96,102,128,134,160,166,192,198,224,230},{1,7,33,39,65,..., dimensions={0} | all-to-all | bytes 262144 | tf_op jit(solution)/shard_map/left_sum/all_to_all | solution.py:187
  36.5 10.7 %all_to_all.22 = f32[16,2,8,128]{3,2,1,0:T(8,128)S(1)} all-to-all(f32[16,2,8,128]{3,2,1,0:T(8,128)S(1)} %left_sum.3), channel_id=1, replica_groups={{0,1,8,9,16,17,24,25,2,3,10,11,18,19,26,27},{6,7,14,15,22,23,30,31,4,5,..., dimensions={0} | all-to-all | bytes 262144 | tf_op jit(solution)/shard_map/left_sum/all_to_all | solution.py:188
  47.2 2.2 %right.1 = (bf16[48,4096]{1,0:T(8,128)(2,1)S(1)}, f32[8,8,448]{2,1,0:T(8,128)S(1)}) custom-call(f32[32,8,128]{2,1,0:T(8,128)S(1)} %bitcast.14, bf16[448,4096]{1,0:T(8,128)(2,1)S(1)} %get-tuple-element.12.gradient, bf16[448,4096]{1,0:T(8,128)(2,1)S(1)} %get-tuple-element.13.feedback), custom_call_target="tpu_custom_call" | custom-call | tf_op jit(solution)/shard_map/right/pallas_call | solution.py:191
  49.4 10.2 %all_to_all.23.rights = f32[8,8,448]{2,1,0:T(8,128)S(1)} all-to-all(f32[8,8,448]{2,1,0:T(8,128)S(1)} %get-tuple-element.14), channel_id=1, replica_groups=mesh['dp'=8,'tensor'=32] {'dp'}, dimensions={0} | all-to-all | bytes 229376 | tf_op jit(solution)/shard_map/right_sum/all_to_all | solution.py:199
  59.6 2.4 %rebuild.1 = (bf16[448,512]{1,0:T(8,128)(2,1)}, bf16[448,4096]{1,0:T(8,128)(2,1)}, f32[8,448]{1,0:T(8,128)}) custom-call(f32[8,8,448]{2,1,0:T(8,128)S(1)} %all_to_all.23.rights, bf16[48,4096]{1,0:T(8,128)(2,1)S(1)} %get-tuple-element.15.basis, bf16[448,4096]{1,0:T(8,128)(2,1)S(1)} %get-tuple-element.12.gradient, bf16[448,4096]{1,0:T(8,128)(2,1)S(1)} %get-tuple-element.13.feedback), custom_call_target="tpu_custom_call" | custom-call | tf_op jit(solution)/shard_map/rebuild/pallas_call | solution.py:201
  (2 shorter events, 0.1 us)

commit v5 on v4

--- a/solution.py
+++ b/solution.py
@@ -12,6 +12,7 @@
 CHUNK = 512
 SIDE = 4
 CORES = 2
+DP_ORDER = [0, 4, 2, 6, 1, 5, 3, 7]
 F32 = jnp.float32
 BF16 = jnp.bfloat16
 LAST_BOTH = (((1,), (1,)), ((), ()))
@@ -141,11 +142,11 @@
 
 def plane_groups(replicas):
     halves = [
-        [(y * SIDE + x) * CORES + core for x in pair for y in range(SIDE) for core in range(CORES)]
+        [(y * SIDE + x) * CORES + core for core in range(CORES) for y in range(SIDE) for x in pair]
         for pair in ((0, 1), (3, 2))
     ]
     parts = SIDE * SIDE * CORES
-    mixed = [[replica * parts + place for replica in range(replicas) for place in pair] for pair in zip(*halves)]
+    mixed = [[replica * parts + place for place in pair for replica in reversed(range(replicas))] for pair in zip(*halves)]
     return halves, mixed
 
 
@@ -196,7 +197,7 @@
             compiler_params=params,
         )(left, gradient, feedback)
     with jax.named_scope("right_sum"):
-        rights = lax.all_to_all(right, "dp", 0, 0)
+        rights = lax.all_to_all(right, "dp", 0, 0, axis_index_groups=[DP_ORDER])
     with jax.named_scope("rebuild"):
         update, residue, right_next = pl.pallas_call(
             functools.partial(rebuild_kernel, replicas),

time: 62.4 us -> 60.2 us (0.965)
  blocking collectives: 53.1 us -> 50.5 us
    all_to_all x1, blocking collectives: 19.3 us -> 17.3 us  [shards(): lax.all_to_all(pieces, ('dp', 'tensor'), 0, 0, axis_index_groups=mixed)]
where the time goes in v5:
time: 60.2 us; the launch traced here: 59.4 us
  blocking collectives  50.5 us (84%)
  Pallas kernels  8.28 us (14%)
  between operations  0.66 us (1%)
    all_to_all x1, blocking collectives, shards(): lax.all_to_all(pieces, ('dp', 'tensor'), 0, 0, axis_index_groups=mixed)  17.3 us
    all_to_all x1, blocking collectives, shards(): lax.all_to_all(pieces, 'tensor', 0, 0, axis_index_groups=halves)  12.5 us
    all_to_all x1, blocking collectives, shards(): left = lax.all_to_all(pieces, 'tensor', 0, 0, axis_index_groups=halves)  10.6 us
    all_to_all x1, blocking collectives, shards(): rights = lax.all_to_all(right, 'dp', 0, 0, axis_index_groups=[DP_ORDER])  10.1 us
    pallas_call x1, Pallas kernels, shards(): pl.pallas_call(left_kernel, out_shape=(jax.ShapeDtypeStruct((wide // LANE...  3.63 us
    pallas_call x1, Pallas kernels, shards(): pl.pallas_call(functools.partial(rebuild_kernel, replicas), out_shape=(ja...  2.42 us
    pallas_call x1, Pallas kernels, shards(): pl.pallas_call(right_kernel, out_shape=(jax.ShapeDtypeStruct((6 * RANK, w...  2.18 us

profile of v5, /device:TPU:1, one launch (start us, length us, event | category | flops | bytes accessed | tf_op | source)
XLA Modules:
  0.0 59.4 jit_solution(5182354605548867250)
XLA Ops:
  0.6 3.6 %left.1 = (f32[32,8,128]{2,1,0:T(8,128)S(1)}, bf16[448,4096]{1,0:T(8,128)(2,1)S(1)}, bf16[448,4096]{1,0:T(8,128)(2,1)S(1)}) custom-call(f32[8,448]{1,0:T(8,128)} %bitcast.18, bf16[448,4096]{1,0:T(8,128)(2,1)} %bitcast.16, bf16[448,4096]{1,0:T(8,128)(2,1)} %bitcast.17), custom_call_target="tpu_custom_call" | custom-call | tf_op jit(solution)/shard_map/left/pallas_call | solution.py:174
  4.3 12.5 %all_to_all.20.pieces = f32[16,2,8,128]{3,2,1,0:T(8,128)S(1)} all-to-all(f32[16,2,8,128]{3,2,1,0:T(8,128)S(1)} %bitcast.15), channel_id=1, replica_groups={{0,2,8,10,16,18,24,26,1,3,9,11,17,19,25,27},{6,4,14,12,22,20,30,28,7,5,..., dimensions={0} | all-to-all | bytes 262144 | tf_op jit(solution)/shard_map/left_sum/all_to_all | solution.py:187
  16.8 17.3 %all_to_all.21.pieces = f32[16,2,8,128]{3,2,1,0:T(8,128)S(1)} all-to-all(f32[16,2,8,128]{3,2,1,0:T(8,128)S(1)} %left_sum.2), channel_id=1, replica_groups={{224,192,160,128,96,64,32,0,230,198,166,134,102,70,38,6},{226,194,162,1..., dimensions={0} | all-to-all | bytes 262144 | tf_op jit(solution)/shard_map/left_sum/all_to_all | solution.py:188
  34.1 10.6 %all_to_all.22 = f32[16,2,8,128]{3,2,1,0:T(8,128)S(1)} all-to-all(f32[16,2,8,128]{3,2,1,0:T(8,128)S(1)} %left_sum.3), channel_id=1, replica_groups={{0,2,8,10,16,18,24,26,1,3,9,11,17,19,25,27},{6,4,14,12,22,20,30,28,7,5,..., dimensions={0} | all-to-all | bytes 262144 | tf_op jit(solution)/shard_map/left_sum/all_to_all | solution.py:189
  44.7 2.2 %right.1 = (bf16[48,4096]{1,0:T(8,128)(2,1)S(1)}, f32[8,8,448]{2,1,0:T(8,128)S(1)}) custom-call(f32[32,8,128]{2,1,0:T(8,128)S(1)} %bitcast.14, bf16[448,4096]{1,0:T(8,128)(2,1)S(1)} %get-tuple-element.12.gradient, bf16[448,4096]{1,0:T(8,128)(2,1)S(1)} %get-tuple-element.13.feedback), custom_call_target="tpu_custom_call" | custom-call | tf_op jit(solution)/shard_map/right/pallas_call | solution.py:192
  46.9 10.1 %all_to_all.23.rights = f32[8,8,448]{2,1,0:T(8,128)S(1)} all-to-all(f32[8,8,448]{2,1,0:T(8,128)S(1)} %get-tuple-element.14), channel_id=1, replica_groups={{0,128,64,192,32,160,96,224},{1,129,65,193,33,161,97,225},{2,130,66,194..., dimensions={0} | all-to-all | bytes 229376 | tf_op jit(solution)/shard_map/right_sum/all_to_all | solution.py:200
  57.0 2.4 %rebuild.1 = (bf16[448,512]{1,0:T(8,128)(2,1)}, bf16[448,4096]{1,0:T(8,128)(2,1)}, f32[8,448]{1,0:T(8,128)}) custom-call(f32[8,8,448]{2,1,0:T(8,128)S(1)} %all_to_all.23.rights, bf16[48,4096]{1,0:T(8,128)(2,1)S(1)} %get-tuple-element.15.basis, bf16[448,4096]{1,0:T(8,128)(2,1)S(1)} %get-tuple-element.12.gradient, bf16[448,4096]{1,0:T(8,128)(2,1)S(1)} %get-tuple-element.13.feedback), custom_call_target="tpu_custom_call" | custom-call | tf_op jit(solution)/shard_map/rebuild/pallas_call | solution.py:202
  (2 shorter events, 0.1 us)

commit v6 on v5

--- a/solution.py
+++ b/solution.py
@@ -142,11 +142,11 @@
 
 def plane_groups(replicas):
     halves = [
-        [(y * SIDE + x) * CORES + core for core in range(CORES) for y in range(SIDE) for x in pair]
+        [(y * SIDE + x) * CORES + core for core in reversed(range(CORES)) for y in reversed(range(SIDE)) for x in pair]
         for pair in ((0, 1), (3, 2))
     ]
     parts = SIDE * SIDE * CORES
-    mixed = [[replica * parts + place for place in pair for replica in reversed(range(replicas))] for pair in zip(*halves)]
+    mixed = [[replica * parts + place for place in reversed(pair) for replica in reversed(range(replicas))] for pair in zip(*halves)]
     return halves, mixed
 
 

time: 60.2 us -> 57.3 us (0.952)
  blocking collectives: 50.5 us -> 48 us
    all_to_all x1, blocking collectives: 17.3 us -> 15.9 us  [shards(): lax.all_to_all(pieces, ('dp', 'tensor'), 0, 0, axis_index_groups=mixed)]
    all_to_all x1, blocking collectives: 12.5 us -> 11.6 us  [shards(): lax.all_to_all(pieces, 'tensor', 0, 0, axis_index_groups=halves)]
where the time goes in v6:
time: 57.3 us; the launch traced here: 56.9 us
  blocking collectives  48 us (84%)
  Pallas kernels  8.28 us (14%)
  between operations  0.66 us (1%)
    all_to_all x1, blocking collectives, shards(): lax.all_to_all(pieces, ('dp', 'tensor'), 0, 0, axis_index_groups=mixed)  15.9 us
    all_to_all x1, blocking collectives, shards(): lax.all_to_all(pieces, 'tensor', 0, 0, axis_index_groups=halves)  11.6 us
    all_to_all x1, blocking collectives, shards(): left = lax.all_to_all(pieces, 'tensor', 0, 0, axis_index_groups=halves)  10.3 us
    all_to_all x1, blocking collectives, shards(): rights = lax.all_to_all(right, 'dp', 0, 0, axis_index_groups=[DP_ORDER])  10.3 us
    pallas_call x1, Pallas kernels, shards(): pl.pallas_call(left_kernel, out_shape=(jax.ShapeDtypeStruct((wide // LANE...  3.63 us
    pallas_call x1, Pallas kernels, shards(): pl.pallas_call(functools.partial(rebuild_kernel, replicas), out_shape=(ja...  2.42 us
    pallas_call x1, Pallas kernels, shards(): pl.pallas_call(right_kernel, out_shape=(jax.ShapeDtypeStruct((6 * RANK, w...  2.18 us

profile of v6, /device:TPU:1, one launch (start us, length us, event | category | flops | bytes accessed | tf_op | source)
XLA Modules:
  0.0 56.9 jit_solution(14897425402955842308)
XLA Ops:
  0.6 3.6 %left.1 = (f32[32,8,128]{2,1,0:T(8,128)S(1)}, bf16[448,4096]{1,0:T(8,128)(2,1)S(1)}, bf16[448,4096]{1,0:T(8,128)(2,1)S(1)}) custom-call(f32[8,448]{1,0:T(8,128)} %bitcast.18, bf16[448,4096]{1,0:T(8,128)(2,1)} %bitcast.16, bf16[448,4096]{1,0:T(8,128)(2,1)} %bitcast.17), custom_call_target="tpu_custom_call" | custom-call | tf_op jit(solution)/shard_map/left/pallas_call | solution.py:174
  4.3 11.6 %all_to_all.20.pieces = f32[16,2,8,128]{3,2,1,0:T(8,128)S(1)} all-to-all(f32[16,2,8,128]{3,2,1,0:T(8,128)S(1)} %bitcast.15), channel_id=1, replica_groups={{25,27,17,19,9,11,1,3,24,26,16,18,8,10,0,2},{31,29,23,21,15,13,7,5,30,2..., dimensions={0} | all-to-all | bytes 262144 | tf_op jit(solution)/shard_map/left_sum/all_to_all | solution.py:187
  15.9 15.9 %all_to_all.21.pieces = f32[16,2,8,128]{3,2,1,0:T(8,128)S(1)} all-to-all(f32[16,2,8,128]{3,2,1,0:T(8,128)S(1)} %left_sum.2), channel_id=1, replica_groups={{255,223,191,159,127,95,63,31,249,217,185,153,121,89,57,25},{253,221,18..., dimensions={0} | all-to-all | bytes 262144 | tf_op jit(solution)/shard_map/left_sum/all_to_all | solution.py:188
  31.7 10.3 %all_to_all.22 = f32[16,2,8,128]{3,2,1,0:T(8,128)S(1)} all-to-all(f32[16,2,8,128]{3,2,1,0:T(8,128)S(1)} %left_sum.3), channel_id=1, replica_groups={{25,27,17,19,9,11,1,3,24,26,16,18,8,10,0,2},{31,29,23,21,15,13,7,5,30,2..., dimensions={0} | all-to-all | bytes 262144 | tf_op jit(solution)/shard_map/left_sum/all_to_all | solution.py:189
  42.0 2.2 %right.1 = (bf16[48,4096]{1,0:T(8,128)(2,1)S(1)}, f32[8,8,448]{2,1,0:T(8,128)S(1)}) custom-call(f32[32,8,128]{2,1,0:T(8,128)S(1)} %bitcast.14, bf16[448,4096]{1,0:T(8,128)(2,1)S(1)} %get-tuple-element.12.gradient, bf16[448,4096]{1,0:T(8,128)(2,1)S(1)} %get-tuple-element.13.feedback), custom_call_target="tpu_custom_call" | custom-call | tf_op jit(solution)/shard_map/right/pallas_call | solution.py:192
  44.2 10.3 %all_to_all.23.rights = f32[8,8,448]{2,1,0:T(8,128)S(1)} all-to-all(f32[8,8,448]{2,1,0:T(8,128)S(1)} %get-tuple-element.14), channel_id=1, replica_groups={{0,128,64,192,32,160,96,224},{1,129,65,193,33,161,97,225},{2,130,66,194..., dimensions={0} | all-to-all | bytes 229376 | tf_op jit(solution)/shard_map/right_sum/all_to_all | solution.py:200
  54.5 2.4 %rebuild.1 = (bf16[448,512]{1,0:T(8,128)(2,1)}, bf16[448,4096]{1,0:T(8,128)(2,1)}, f32[8,448]{1,0:T(8,128)}) custom-call(f32[8,8,448]{2,1,0:T(8,128)S(1)} %all_to_all.23.rights, bf16[48,4096]{1,0:T(8,128)(2,1)S(1)} %get-tuple-element.15.basis, bf16[448,4096]{1,0:T(8,128)(2,1)S(1)} %get-tuple-element.12.gradient, bf16[448,4096]{1,0:T(8,128)(2,1)S(1)} %get-tuple-element.13.feedback), custom_call_target="tpu_custom_call" | custom-call | tf_op jit(solution)/shard_map/rebuild/pallas_call | solution.py:202
  (2 shorter events, 0.1 us)
